TPU v7x, 32 devices: a whole 2x2x4 slice. The times are simulated.
32 devices in a mesh: dp: 4 (over y, x), ctx: 8 (over z, core).
Axes of the slice: x: 2, y: 2, z: 4, core: 2. Of those that a mesh axis runs over, the one named last changes fastest.
Arguments:
- inputs: bfloat16 [8192, 8192], P(('dp', 'ctx')), parts along dimension 0, may hold values from -6 to 6
- key_query: bfloat16 [8192, 2048], P(('dp', 'ctx')), parts along dimension 0, may hold values from -3 to 3
- conv_inputs: float32 [4, 8192], replicated, may hold values from -3 to 3
- conv_kq: float32 [4, 2048], replicated, may hold values from -3 to 3
- step_size: float32 [8192, 128], P(('dp', 'ctx')), parts along dimension 0, may hold values from 0.1 to 1
- decay_log: float32 [8192, 128], P(('dp', 'ctx')), parts along dimension 0, may hold values from -1 to 0, as said below
- skip_gain: float32 [128], replicated, may hold values from 0.5 to 1.5
- norm_gain: float32 [8192], replicated, may hold values from 0.5 to 1.5
Outputs:
- mixed: bfloat16 [8192, 8192], P('dp', 'ctx'), parts along dimension 0
There are 4 independent parts, one for each index of `dp`. A program takes and returns all parts, laid end to end along the dimension named above; an argument that names none is the same for every part. Nothing has to cross between parts.
Inputs may be any that keep to these rules, and one draw needn't show every extreme that they name: `decay_log`: log decay factors, all negative.
All inputs are finite; a program needn't handle non-finite values.
Results may differ from a plain program's by a relative error of at most 0.0085.
Values may be sent and summed in bfloat16 or wider, within the bound.
No kernel may reach another device: no remote copies, remote signals or barrier semaphores. Data moves between devices by JAX's collectives and lax.ppermute only.
A program may use at most 448 MiB of HBM per device.

v0:
```python
import functools
import math

import jax
import jax.numpy as jnp
import numpy as np
from jax import lax
from jax.experimental import pallas as pl
from jax.experimental.pallas import tpu as pltpu
from jax.sharding import PartitionSpec as P

HEADS = 128
HEAD_DIM = 64
STATE = 128
GROUPS = 8
KW = 4
BLOCK = 128
GROUP_WIDTH = HEADS * HEAD_DIM // GROUPS
EPS = 1e-05
HALO = 16
LANES = 128
SUBLANES = 8
FIELDS = 2
ROUND_ORDER = (0, 1, 2, 4, 3, 5, 6, 7)
STRIP = 64
PACK_VMEM = 58 * 1024 * 1024
VMEM_LIMIT = 32 * 1024 * 1024


def contract(a, b, dims):
    return lax.dot_general(a, b, (dims, ((), ())), preferred_element_type=jnp.float32)


def as_parts(v, count):
    parts = []
    for _ in range(count):
        part = v.astype(jnp.bfloat16)
        parts.append(part)
        v = v - part.astype(jnp.float32)
    return parts


def scalar_units(heads, rows, cols):
    units = []
    for p in range(FIELDS):
        for head in range(0, heads, SUBLANES):
            line, column = divmod(len(units), cols // rows)
            units.append((p, head, min(SUBLANES, heads), line * SUBLANES, column * rows))
    return units


def pack_kernel(peers, span, widths, heads, entries, scalar_rows, *refs):
    refs = list(refs)
    owner_ref = refs.pop(0)
    x_ref = refs.pop(0)
    heading = scalar_rows > 0
    if heading:
        kq_ref, decay_ref, step_ref = refs[:3]
        del refs[:3]
    outs = refs[: len(entries)]
    del refs[: len(entries)]
    if heading:
        raw_scalars, scalars, kq_near = refs[:3]
    sems = refs[-1]
    rows = x_ref.shape[0]
    owned = HEADS * HEAD_DIM // peers
    lead = widths[0] + 2 * STATE
    copies = []
    if heading:
        loads = [
            pltpu.make_async_copy(ref, raw_scalars.at[i], sems.at[2, i])
            for i, ref in enumerate((decay_ref, step_ref))
        ]
        loads.append(pltpu.make_async_copy(kq_ref, kq_near, sems.at[2, 2]))
        for load in loads:
            load.start()
    owners = [owner_ref[code] for code, _ in entries]
    for i, (owner, (_, kind)) in enumerate(zip(owners, entries)):
        pieces = {
            "full": [(0, 0, 0), (1, widths[0], lead)],
            "lead": [(0, 0, 0)],
            "rest": [(1, widths[0], 0)],
        }[kind]
        for index, offset, left in pieces:
            column = pl.multiple_of(owner * owned + offset, LANES)
            copies.append(
                pltpu.make_async_copy(
                    x_ref.at[:, pl.ds(column, widths[index])],
                    outs[i].at[0:rows, left : left + widths[index]],
                    sems.at[index, i],
                )
            )
    for copy in copies:
        copy.start()
    if heading:
        for load in loads:
            load.wait()
        fields = [raw_scalars[0].T, raw_scalars[1].T]
        for p, field in enumerate(fields):
            for owner in range(peers):
                scalars[p, owner] = field[owner * heads : (owner + 1) * heads]
        for i, owner in enumerate(owners):
            outs[i][rows:] = jnp.zeros((scalar_rows, outs[i].shape[1]), jnp.bfloat16)
            for p, head, count, top, left in scalar_units(heads, rows, lead):
                outs[i][rows + top : rows + top + count, left : left + rows] = scalars[
                    p, owner, head : head + count
                ].astype(jnp.bfloat16)
            for j in range(2):
                column = pl.multiple_of((j * GROUPS + owner // span) * STATE, LANES)
                left = widths[0] + j * STATE
                outs[i][0:rows, left : left + STATE] = kq_near[:, pl.ds(column, STATE)]
    for copy in copies:
        copy.wait()


def mixer_kernel(peers, rows, heads, chunk, widths, whole_group, *refs):
    refs = list(refs)

    def take(count):
        taken = refs[:count]
        del refs[:count]
        return taken

    first = chunk == 0
    final = chunk == len(widths) - 1 and whole_group
    later = range(1, len(widths)) if first else ()
    width = widths[chunk]
    (slot_ref,) = take(1)
    parts = take(peers)
    taps_ref, skip_ref = take(2)
    if not first:
        left_ref, b_ref, inward_ref, outward_ref, power_ref = take(5)
    if final:
        (gain_ref,) = take(1)
        earlier = take(chunk)
        (out_ref,) = take(1)
    else:
        total_ref, sums_ref = take(2)
    if first and later:
        left_ref, b_ref = take(2)
        inward_refs = take(len(later))
        outward_refs = take(len(later))
    wide, carry = take(2)
    if final:
        (total_ref,) = take(1)
    if first:
        (scalars,) = take(1)
    blocks = rows // BLOCK
    step = pl.program_id(0)
    scale_rows = rows + 16 * blocks
    base = pl.multiple_of(step * rows, rows)
    scale_base = pl.multiple_of(step * scale_rows, 32)

    @pl.when(step == 0)
    def _():
        carry[...] = jnp.zeros_like(carry)
        wide[rows : rows + HALO] = jnp.zeros((HALO, wide.shape[1]), jnp.bfloat16)

    wide[0:HALO] = wide[rows : rows + HALO]
    slot = slot_ref[step]
    for k in range(peers):

        @pl.when(slot == k)
        def _():
            if first:
                wide[HALO : HALO + rows] = parts[k][0:rows, 0 : wide.shape[1]]
                scalars[...] = parts[k][rows:, 0 : wide.shape[1]]
            else:
                wide[HALO : HALO + rows] = parts[k][0:rows, parts[k].shape[1] - width :]

    def spread(count):
        head_of = lax.broadcasted_iota(jnp.int32, (2 * count, count * HEAD_DIM), 1) // HEAD_DIM
        row = lax.rem(
            lax.broadcasted_iota(jnp.int32, (2 * count, count * HEAD_DIM), 0), count
        )
        return jnp.where(head_of == row, 1.0, 0.0).astype(jnp.bfloat16)

    def activated(top, size, lo, hi):
        rows_out = []
        for r in range(top, top + size, STRIP):
            lanes_out = []
            for lane in range(lo, hi, LANES):
                tap = [taps_ref[k : k + 1, lane : lane + LANES] for k in range(KW)]
                now = wide[r : r + STRIP + HALO, lane : lane + LANES].astype(jnp.float32)[HALO // 2 :]
                before = pltpu.roll(now, 1, 0)
                older = pltpu.roll(tap[0] * before + tap[1] * now, 2, 0)
                summed = (older + (tap[2] * before + tap[3] * now))[HALO // 2 :]
                lanes_out.append(
                    summed * pltpu.reciprocal(1.0 + jnp.exp(-summed), approx=True)
                )
            rows_out.append(jnp.concatenate(lanes_out, axis=1))
        return jnp.concatenate(rows_out, axis=0)

    if first:
        full = width + 2 * STATE
        row = lax.broadcasted_iota(jnp.int32, (rows, rows), 0)
        col = lax.broadcasted_iota(jnp.int32, (rows, rows), 1)
        lower = (row >= col) & (row // BLOCK == col // BLOCK)
        ones = jnp.where(lower, 1.0, 0.0).astype(jnp.bfloat16)
        eye = jnp.where(row == col, 1.0, 0.0).astype(jnp.bfloat16)

        def field(p):
            pieces = [
                scalars[top : top + count, left : left + rows].astype(jnp.float32)
                for q, _, count, top, left in scalar_units(heads, rows, full)
                if q == p
            ]
            return jnp.concatenate(pieces, axis=0).astype(jnp.bfloat16)

        cumul = contract(ones, field(0), ((1,), (1,)))
        steps = contract(eye, field(1), ((1,), (1,)))
        middles = [
            cumul[b * BLOCK + BLOCK // 2 - 1 : b * BLOCK + BLOCK // 2] for b in range(blocks)
        ]
        middle = jnp.concatenate([jnp.broadcast_to(m, (BLOCK, heads)) for m in middles], axis=0)
        inward = as_parts(steps * jnp.exp(middle - cumul), 2)
        outward = as_parts(
            jnp.concatenate(
                [jnp.exp(cumul - middle)]
                + [jnp.broadcast_to(jnp.exp(m), (16, heads)) for m in middles],
                axis=0,
            ),
            2,
        )

        def chosen(halves, index):
            begin = sum(widths[:index]) // HEAD_DIM
            end = begin + widths[index] // HEAD_DIM
            return jnp.concatenate([half[:, begin:end] for half in halves], axis=1)

        bc = activated(0, rows, width, full).astype(jnp.bfloat16)
        b_part, c_part = bc[:, :STATE], bc[:, STATE:]
        scores = contract(c_part, b_part, ((1,), (1,)))
        scores = jnp.where(lower, scores, 0.0).astype(jnp.bfloat16)
        lefts = [
            jnp.concatenate(
                [
                    scores[b * BLOCK : (b + 1) * BLOCK, b * BLOCK : (b + 1) * BLOCK],
                    c_part[b * BLOCK : (b + 1) * BLOCK],
                ],
                axis=1,
            )
            for b in range(blocks)
        ]
        for index in later:
            inward_refs[index - 1][pl.ds(base, rows)] = chosen(inward, index)
            outward_refs[index - 1][pl.ds(scale_base, scale_rows)] = chosen(outward, index)
        if later:
            b_ref[pl.ds(base, rows)] = b_part
            for b in range(blocks):
                left_ref[pl.ds(base + b * BLOCK, BLOCK)] = lefts[b]
        inward = chosen(inward, 0)
        outward = chosen(outward, 0)
    else:
        inward = inward_ref[pl.ds(base, rows)]
        outward = outward_ref[pl.ds(scale_base, scale_rows)]
        b_part = b_ref[pl.ds(base, rows)]
        lefts = [left_ref[pl.ds(base + b * BLOCK, BLOCK)] for b in range(blocks)]

    tile = 2 * LANES if width % (2 * LANES) == 0 else LANES
    expand = spread(width // HEAD_DIM)
    compact = [
        jnp.concatenate(
            [
                inward[b * BLOCK : (b + 1) * BLOCK],
                outward[b * BLOCK : (b + 1) * BLOCK],
                outward[rows + 16 * b : rows + 16 * (b + 1)],
            ],
            axis=0,
        )
        for b in range(blocks)
    ]
    for b in range(blocks):
        top = b * BLOCK
        power = jnp.zeros((BLOCK, LANES), jnp.float32)
        if not first:
            power = power_ref[pl.ds(base + top, BLOCK)]
        for lo in range(0, width, tile):
            hi = lo + tile
            x_conv = activated(top, BLOCK, lo, hi)
            scales = contract(compact[b], expand[:, lo:hi], ((1,), (0,)))
            in_scale = scales[:BLOCK]
            out_scale = scales[BLOCK : 2 * BLOCK]
            mid_scale = scales[2 * BLOCK :]
            scaled = (x_conv * in_scale).astype(jnp.bfloat16)
            held = carry[:, lo:hi] * mid_scale[0:1]
            right = jnp.concatenate([scaled, held.astype(jnp.bfloat16)], axis=0)
            mixed = contract(lefts[b], right, ((1,), (0,)))
            total = mixed * out_scale + skip_ref[0:1, lo:hi] * x_conv
            if final:
                total_ref[top : top + BLOCK, lo:hi] = total
            else:
                total_ref[pl.ds(base + top, BLOCK), lo:hi] = total.astype(jnp.bfloat16)
            squares = total * total
            for lane in range(0, tile, LANES):
                power = power + squares[:, lane : lane + LANES]
            added = contract(b_part[top : top + BLOCK], scaled, ((0,), (0,)))
            carry[:, lo:hi] = (held + added) * out_scale[BLOCK - 1 : BLOCK]
        if final:
            summed = jnp.sum(power, axis=1, keepdims=True)
            norm = lax.rsqrt(summed * (1.0 / GROUP_WIDTH) + EPS)
            column = 0
            for index, size in enumerate(widths):
                if index < chunk:
                    block = earlier[index][pl.ds(base + top, BLOCK)].astype(jnp.float32)
                else:
                    block = total_ref[top : top + BLOCK]
                out_ref[top : top + BLOCK, column : column + size] = (
                    block * norm * gain_ref[0:1, column : column + size]
                ).astype(jnp.bfloat16)
                column += size
        else:
            sums_ref[pl.ds(base + top, BLOCK)] = power


def per_device(inputs, key_query, conv_inputs, conv_kq, step_size, decay_log, skip_gain, norm_gain):
    peers = lax.axis_size("ctx")
    me = lax.axis_index("ctx")
    position = np.arange(peers)
    if peers == len(ROUND_ORDER):
        position = np.argsort(ROUND_ORDER)
    steps = np.arange(peers)
    owner_table = np.argsort(position)[(position[:, None] + steps) % peers].astype(np.int32)
    slot_table = ((position[:, None] - position) % peers).astype(np.int32)
    owners = lax.dynamic_index_in_dim(jnp.asarray(owner_table), me, 0, False)
    slots = lax.dynamic_index_in_dim(jnp.asarray(slot_table), me, 0, False)
    rows = inputs.shape[0]
    owned = HEADS * HEAD_DIM // peers
    heads = HEADS // peers
    span = GROUP_WIDTH // owned
    whole_group = span == 1
    total_rows = peers * rows
    blocks = rows // BLOCK
    tiles = owned // LANES
    last = max(1, tiles // 4)
    widths = [(tiles - last) * LANES, last * LANES]
    offsets = [0, widths[0]]

    smem = pl.BlockSpec(memory_space=pltpu.SMEM)
    hbm = pl.BlockSpec(memory_space=pltpu.HBM)
    vmem = pl.BlockSpec(memory_space=pltpu.VMEM)
    params = pltpu.CompilerParams(vmem_limit_bytes=VMEM_LIMIT)

    def columns(a, first, size):
        return lax.dynamic_slice_in_dim(a, first, size, axis=1)

    lead_cols = widths[0] + 2 * STATE
    scalar_rows = scalar_units(heads, rows, lead_cols)[-1][3] + SUBLANES
    extents = {
        "full": (rows + scalar_rows, lead_cols + widths[1]),
        "lead": (rows + scalar_rows, lead_cols),
        "rest": (rows, widths[1]),
    }

    def pack(entries):
        heading = entries[0][1] != "rest"
        shapes = [jax.ShapeDtypeStruct(extents[kind], jnp.bfloat16) for _, kind in entries]
        operands = [owners, inputs]
        in_specs = [smem, hbm]
        scratch = []
        if heading:
            operands += [key_query, decay_log, step_size]
            in_specs += [hbm] * 3
            scratch.append(pltpu.VMEM((2, rows, HEADS), jnp.float32))
            scratch.append(pltpu.VMEM((FIELDS, peers, heads, rows), jnp.float32))
            scratch.append(pltpu.VMEM(key_query.shape, jnp.bfloat16))
        scratch.append(pltpu.SemaphoreType.DMA((3, max(3, len(entries)))))
        return pl.pallas_call(
            functools.partial(
                pack_kernel,
                peers,
                span,
                widths,
                heads,
                entries,
                scalar_rows if heading else 0,
            ),
            in_specs=in_specs,
            out_specs=[vmem] * len(entries),
            out_shape=shapes,
            scratch_shapes=scratch,
            compiler_params=pltpu.CompilerParams(vmem_limit_bytes=PACK_VMEM),
            cost_estimate=pl.CostEstimate(
                flops=0,
                bytes_accessed=4 * sum(math.prod(shape.shape) for shape in shapes),
                transcendentals=0,
            ),
            name="pack",
        )(*operands)

    def send(message, code, after=()):
        message, _ = lax.optimization_barrier((message, after))
        pairs = [(i, int(owner_table[i, code])) for i in range(peers)]
        return lax.ppermute(message, "ctx", pairs)

    far = sorted(range(2, peers - 1), key=lambda code: abs(code - peers // 2))
    near = [1, peers - 1]
    kinds = [(code, "lead") for code in far] + [(code, "full") for code in near + [0]]
    lead = {code: message for (code, _), message in zip(kinds, pack(kinds))}
    rest = {code: lead[code] for code in near + [0]}
    rest.update(zip(far, pack([(code, "rest") for code in far])))
    for code in far + near:
        lead[code] = send(lead[code], code)
    for code in far:
        rest[code] = send(rest[code], code, [lead[other] for other in far + near])
    for code in near:
        rest[code] = lead[code]
    received = [[parts[code] for code in range(peers)] for parts in (lead, rest)]

    taps_x = columns(conv_inputs, me * owned, owned)
    group = me // span
    taps_kq = jnp.concatenate(
        [
            columns(conv_kq, group * STATE, STATE),
            columns(conv_kq, (GROUPS + group) * STATE, STATE),
        ],
        axis=1,
    )
    skip = jnp.repeat(lax.dynamic_slice_in_dim(skip_gain, me * heads, heads), HEAD_DIM)[None]
    gain = columns(norm_gain[None], me * owned, owned)

    def by_source(count, lanes, dtype):
        spec = pl.BlockSpec((count, lanes), lambda i: (i, 0))
        return spec, jax.ShapeDtypeStruct((peers * count, lanes), dtype)

    def whole(count, lanes, dtype):
        return vmem, jax.ShapeDtypeStruct((peers * count, lanes), dtype)

    totals = []
    power = None
    shared = None
    for chunk, width in enumerate(widths):
        first = chunk == 0
        final = chunk == len(widths) - 1 and whole_group
        taps = taps_x[:, offsets[chunk] : offsets[chunk] + width]
        if first:
            taps = jnp.concatenate([taps, taps_kq], axis=1)
        cols = taps.shape[1]
        operands = [slots, *received[chunk], taps, skip[:, offsets[chunk] : offsets[chunk] + width]]
        if not first:
            left, b_part, inward, outward = shared
            operands += [left, b_part, inward[chunk - 1], outward[chunk - 1], power]
        if final:
            operands += [gain, *totals]
        out = []
        if final:
            out.append(by_source(rows, owned, jnp.bfloat16))
        else:
            out.append(whole(rows, width, jnp.bfloat16))
            out.append(whole(rows, LANES, jnp.float32))
        if first:
            out.append(whole(rows, 2 * STATE, jnp.bfloat16))
            out.append(whole(rows, STATE, jnp.bfloat16))
            for count in (rows, rows + 16 * blocks):
                for size in widths[1:]:
                    out.append(whole(count, 2 * size // HEAD_DIM, jnp.bfloat16))
        scratch = [
            pltpu.VMEM((rows + HALO, cols), jnp.bfloat16),
            pltpu.VMEM((STATE, width), jnp.float32),
        ]
        if final:
            scratch.append(pltpu.VMEM((rows, width), jnp.float32))
        if first:
            scratch.append(pltpu.VMEM((scalar_rows, cols), jnp.bfloat16))
        results = pl.pallas_call(
            functools.partial(mixer_kernel, peers, rows, heads, chunk, widths, whole_group),
            grid=(peers,),
            in_specs=[smem] + [vmem] * (len(operands) - 1),
            out_specs=[spec for spec, _ in out],
            out_shape=[shape for _, shape in out],
            scratch_shapes=scratch,
            compiler_params=params,
            cost_estimate=pl.CostEstimate(
                flops=2 * total_rows * width * 450,
                bytes_accessed=total_rows * (2 * cols + 8 * width),
                transcendentals=total_rows * cols,
            ),
            name=f"mixer{chunk}",
        )(*operands)
        if final:
            return results[0]
        totals.append(results[0])
        power = results[1]
        if first:
            rest = results[4:]
            shared = (results[2], results[3], rest[: len(rest) // 2], rest[len(rest) // 2 :])
    sharers = [list(range(i, i + span)) for i in range(0, peers, span)]
    summed = jnp.sum(power, axis=1, keepdims=True)
    summed = lax.psum(summed, "ctx", axis_index_groups=sharers)
    total = jnp.concatenate(totals, axis=1)
    return (total * lax.rsqrt(summed * (1.0 / GROUP_WIDTH) + EPS) * gain).astype(jnp.bfloat16)


def solution(mesh):
    in_specs = (
        P(("dp", "ctx"), None),
        P(("dp", "ctx"), None),
        P(),
        P(),
        P(("dp", "ctx"), None),
        P(("dp", "ctx"), None),
        P(),
        P(),
    )
    out_specs = P("dp", "ctx")
    return jax.shard_map(
        per_device, mesh=mesh, in_specs=in_specs, out_specs=out_specs, check_vma=False
    )
```

profile of v0, /device:TPU:12, one launch (start us, length us, event | category | flops | bytes accessed | tf_op | source)
XLA Modules:
  0.0 140.4 jit_solution(3315041900549998243)
XLA Ops:
  0.0 0.0 copy-start
  0.0 0.0 copy-start.2
  0.0 1.2 fusion.1.refs_0_
  1.3 5.5 %pack.2 = (bf16[264,1024]{1,0:T(8,128)(2,1)}, bf16[264,1024]{1,0:T(8,128)(2,1)}, bf16[264,1024]{1,0:T(8,128)(2,1)}, bf16[264,1024]{1,0:T(8,128)(2,1)}, bf16[264,...) custom-call(s32[8]{0:T(128)} %fusion.1.refs_0_, ...), custom_call_target="tpu_custom_call" | custom-call | bytes 9461760 | tf_op jit(solution)/shard_map/pack/pallas_call | solution.py:368
  6.7 0.0 copy-start.1
  6.7 2.7 %collective-permute-start.1 = (bf16[264,1024]{1,0:T(8,128)(2,1)}, bf16[264,1024]{1,0:T(8,128)(2,1)S(1)}, u32[]{:S(2)}, u32[]{:S(2)}) collective-permute-start(bf16[264,1024]{1,0:T(8,128)(2,1)} %get-tuple-element.32), channel_id=1, source_target_pairs={{0,3},{1,5},{2,6},{3,0},{4,7},{5,1},{6,2},{7,4},{8,11},{9,13},{10,... | collective-permute-start | bytes 1622024 | tf_op jit(solution)/shard_map/ppermute | solution.py:394
  9.4 0.0 collective-permute-start.2
  9.4 0.9 collective-permute-start
  10.3 0.8 collective-permute-start.6
  11.1 1.8 %collective-permute-start.3 = (bf16[264,1024]{1,0:T(8,128)(2,1)}, bf16[264,1024]{1,0:T(8,128)(2,1)}, u32[]{:S(2)}, u32[]{:S(2)}) collective-permute-start(bf16[264,1024]{1,0:T(8,128)(2,1)} %get-tuple-element.34), channel_id=1, source_target_pairs={{0,5},{1,6},{2,7},{3,1},{4,0},{5,2},{6,4},{7,3},{8,13},{9,14},{10,... | collective-permute-start | bytes 1622024 | tf_op jit(solution)/shard_map/ppermute | solution.py:394
  12.9 0.0 copy-done.2
  12.9 0.1 dynamic_slice.25
  13.0 0.1 broadcast_in_dim.4
  13.1 0.1 broadcast_in_dim_reshape.3
  13.2 2.8 %pack.3 = (bf16[256,256]{1,0:T(8,128)(2,1)}, bf16[256,256]{1,0:T(8,128)(2,1)}, bf16[256,256]{1,0:T(8,128)(2,1)}, bf16[256,256]{1,0:T(8,128)(2,1)}, bf16[256,256]{1,0:T(8,128)(2,1)}) custom-call(s32[8]{0:T(128)} %fusion.1.refs_0_, bf16[256,8192]{1,0:T(8,128)(2,1)} %refs_1_.3), custom_call_target="tpu_custom_call" | custom-call | bytes 1310720 | tf_op jit(solution)/shard_map/pack/pallas_call | solution.py:368
  16.0 0.7 dynamic-slice.3
  16.7 17.5 %collective-permute-done.1.refs_5_ = bf16[264,1024]{1,0:T(8,128)(2,1)S(1)} collective-permute-done((bf16[264,1024]{1,0:T(8,128)(2,1)}, bf16[264,1024]{1,0:T(8,128)(2,1)S(1)}, u32[]{:S(2)}, u32[]{:S(2)}) %collective-permute-start.1) | collective-permute-done | bytes 540704 | tf_op jit(solution)/shard_map/ppermute | solution.py:394
  34.3 0.0 collective-permute-start.4
  34.3 34.0 %collective-permute-done.2.refs_4_ = bf16[264,1024]{1,0:T(8,128)(2,1)S(1)} collective-permute-done((bf16[264,1024]{1,0:T(8,128)(2,1)}, bf16[264,1024]{1,0:T(8,128)(2,1)S(1)}, u32[]{:S(2)}, u32[]{:S(2)}) %collective-permute-start.2) | collective-permute-done | bytes 540704 | tf_op jit(solution)/shard_map/ppermute | solution.py:394
  68.3 0.0 collective-permute-start.5
  68.3 0.7 fusion.refs_0_
  69.0 0.0 copy-done
  69.0 0.7 constant_dynamic-slice_fusion.2
  69.7 37.5 %collective-permute-done.3.refs_6_ = bf16[264,1024]{1,0:T(8,128)(2,1)} collective-permute-done((bf16[264,1024]{1,0:T(8,128)(2,1)}, bf16[264,1024]{1,0:T(8,128)(2,1)}, u32[]{:S(2)}, u32[]{:S(2)}) %collective-permute-start.3) | collective-permute-done | bytes 540704 | tf_op jit(solution)/shard_map/ppermute | solution.py:394
  107.2 0.0 collective-permute-done.4.refs_3_
  107.2 0.0 collective-permute-done.5.refs_7_
  107.2 0.0 collective-permute-done.refs_2_
  107.2 0.0 collective-permute-done.6.refs_8_
  107.2 1.4 %collective-permute-start.7 = (bf16[256,256]{1,0:T(8,128)(2,1)}, bf16[256,256]{1,0:T(8,128)(2,1)S(1)}, u32[]{:S(2)}, u32[]{:S(2)}) collective-permute-start(bf16[256,256]{1,0:T(8,128)(2,1)} %get-tuple-element.38), channel_id=1, source_target_pairs={{0,2},{1,4},{2,3},{3,6},{4,5},{5,7},{6,0},{7,1},{8,10},{9,12},{10,... | collective-permute-start | bytes 393224 | tf_op jit(solution)/shard_map/ppermute | solution.py:394
  108.6 1.9 %collective-permute-start.8 = (bf16[256,256]{1,0:T(8,128)(2,1)}, bf16[256,256]{1,0:T(8,128)(2,1)S(1)}, u32[]{:S(2)}, u32[]{:S(2)}) collective-permute-start(bf16[256,256]{1,0:T(8,128)(2,1)} %get-tuple-element.40), channel_id=1, source_target_pairs={{0,4},{1,3},{2,5},{3,7},{4,6},{5,0},{6,1},{7,2},{8,12},{9,11},{10,... | collective-permute-start | bytes 393224 | tf_op jit(solution)/shard_map/ppermute | solution.py:394
  110.6 1.4 collective-permute-start.9
  111.9 1.7 %collective-permute-start.10 = (bf16[256,256]{1,0:T(8,128)(2,1)}, bf16[256,256]{1,0:T(8,128)(2,1)S(1)}, u32[]{:S(2)}, u32[]{:S(2)}) collective-permute-start(bf16[256,256]{1,0:T(8,128)(2,1)} %get-tuple-element.44), channel_id=1, source_target_pairs={{0,5},{1,6},{2,7},{3,1},{4,0},{5,2},{6,4},{7,3},{8,13},{9,14},{10,... | collective-permute-start | bytes 393224 | tf_op jit(solution)/shard_map/ppermute | solution.py:394
  113.6 2.3 %collective-permute-start.11 = (bf16[256,256]{1,0:T(8,128)(2,1)}, bf16[256,256]{1,0:T(8,128)(2,1)S(1)}, u32[]{:S(2)}, u32[]{:S(2)}) collective-permute-start(bf16[256,256]{1,0:T(8,128)(2,1)} %get-tuple-element.46), channel_id=1, source_target_pairs={{0,6},{1,7},{2,0},{3,2},{4,1},{5,4},{6,3},{7,5},{8,14},{9,15},{10,... | collective-permute-start | bytes 393224 | tf_op jit(solution)/shard_map/ppermute | solution.py:394
  115.9 0.0 copy-done.1
  115.9 16.6 %mixer0.1 = (bf16[2048,768]{1,0:T(8,128)(2,1)S(1)}, f32[2048,128]{1,0:T(8,128)S(1)}, bf16[2048,256]{1,0:T(8,128)(2,1)S(1)}, bf16[2048,128]{1,0:T(8,128)(2,1)S(1)...) custom-call(s32[8]{0:T(128)S(1)} %fusion.refs_0_, bf16[264,1280]{1,0:T(8,128)(2,1)S(1)} %copy-done.1, ...), custom_call_target="tpu_custom_call" | custom-call | flops 1415577600 | bytes 16777216 | tf_op jit(solution)/shard_map/mixer0/pallas_call | solution.py:465
  132.5 0.0 collective-permute-done.7.refs_3_
  132.5 0.0 collective-permute-done.8.refs_4_
  132.5 0.0 collective-permute-done.9.refs_5_
  132.6 0.0 collective-permute-done.10.refs_6_
  132.6 0.0 collective-permute-done.11.refs_7_
  132.6 7.9 %mixer1.1 = bf16[2048,1024]{1,0:T(8,128)(2,1)} custom-call(s32[8]{0:T(128)S(1)} %fusion.refs_0_, bf16[264,1280]{1,0:T(8,128)(2,1)S(1)} %copy-done.1, bf16[264,1280]{1,0:T(8,128)(2,1)S(1)} %collective-permute-done.refs_2_, bf16[256,256]{1,0:T(8,128)(2,1)S(1)} %collective-permute-done.7.refs_3_, bf16[256,256]{1,0:T(8,128)(2,1)S(1)} %collective-permute-done.8.refs_4_, ...), custom_call_target="tpu_custom_call" | custom-call | flops 471859200 | bytes 5242880 | tf_op jit(solution)/shard_map/mixer1/pallas_call | solution.py:465
  (5 shorter events, 0.0 us)
Async XLA Ops:
  0.0 69.0 %copy-start = (f32[4,8192]{1,0:T(4,128)S(1)}, f32[4,8192]{1,0:T(4,128)}, u32[]{:S(2)}) copy-start(f32[4,8192]{1,0:T(4,128)} %param.12) | copy-start | bytes 393220
  0.0 12.9 %copy-start.2 = (f32[128]{0:T(128)S(1)}, f32[128]{0:T(128)}, u32[]{:S(2)}) copy-start(f32[128]{0:T(128)} %param.16) | copy-start | bytes 1540
  6.7 109.2 %copy-start.1 = (bf16[264,1280]{1,0:T(8,128)(2,1)S(1)}, bf16[264,1280]{1,0:T(8,128)(2,1)}, u32[]{:S(2)}) copy-start(bf16[264,1280]{1,0:T(8,128)(2,1)} %get-tuple-element.29.refs_1_) | copy-start | bytes 2027524
  6.7 27.5 %collective-permute-start.1 = (bf16[264,1024]{1,0:T(8,128)(2,1)}, bf16[264,1024]{1,0:T(8,128)(2,1)S(1)}, u32[]{:S(2)}, u32[]{:S(2)}) collective-permute-start(bf16[264,1024]{1,0:T(8,128)(2,1)} %get-tuple-element.32), channel_id=1, source_target_pairs={{0,3},{1,5},{2,6},{3,0},{4,7},{5,1},{6,2},{7,4},{8,11},{9,13},{10,... | collective-permute-start | bytes 1622024 | tf_op jit(solution)/shard_map/ppermute | solution.py:394
  9.4 58.9 %collective-permute-start.2 = (bf16[264,1024]{1,0:T(8,128)(2,1)}, bf16[264,1024]{1,0:T(8,128)(2,1)S(1)}, u32[]{:S(2)}, u32[]{:S(2)}) collective-permute-start(bf16[264,1024]{1,0:T(8,128)(2,1)} %get-tuple-element.33), channel_id=1, source_target_pairs={{0,4},{1,3},{2,5},{3,7},{4,6},{5,0},{6,1},{7,2},{8,12},{9,11},{10,... | collective-permute-start | bytes 1622024 | tf_op jit(solution)/shard_map/ppermute | solution.py:394
  9.4 97.8 %collective-permute-start = (bf16[264,1280]{1,0:T(8,128)(2,1)}, bf16[264,1280]{1,0:T(8,128)(2,1)S(1)}, u32[]{:S(2)}, u32[]{:S(2)}) collective-permute-start(bf16[264,1280]{1,0:T(8,128)(2,1)} %get-tuple-element.30), channel_id=1, source_target_pairs={{0,1},{1,2},{2,4},{3,5},{4,3},{5,6},{6,7},{7,0},{8,9},{9,10},{10,1... | collective-permute-start | bytes 2027528 | tf_op jit(solution)/shard_map/ppermute | solution.py:394
  10.3 96.9 %collective-permute-start.6 = (bf16[264,1280]{1,0:T(8,128)(2,1)}, bf16[264,1280]{1,0:T(8,128)(2,1)S(1)}, u32[]{:S(2)}, u32[]{:S(2)}) collective-permute-start(bf16[264,1280]{1,0:T(8,128)(2,1)} %get-tuple-element.37), channel_id=1, source_target_pairs={{0,7},{1,0},{2,1},{3,4},{4,2},{5,3},{6,5},{7,6},{8,15},{9,8},{10,9... | collective-permute-start | bytes 2027528 | tf_op jit(solution)/shard_map/ppermute | solution.py:394
  11.1 96.1 %collective-permute-start.3 = (bf16[264,1024]{1,0:T(8,128)(2,1)}, bf16[264,1024]{1,0:T(8,128)(2,1)}, u32[]{:S(2)}, u32[]{:S(2)}) collective-permute-start(bf16[264,1024]{1,0:T(8,128)(2,1)} %get-tuple-element.34), channel_id=1, source_target_pairs={{0,5},{1,6},{2,7},{3,1},{4,0},{5,2},{6,4},{7,3},{8,13},{9,14},{10,... | collective-permute-start | bytes 1622024 | tf_op jit(solution)/shard_map/ppermute | solution.py:394
  34.3 73.0 %collective-permute-start.4 = (bf16[264,1024]{1,0:T(8,128)(2,1)}, bf16[264,1024]{1,0:T(8,128)(2,1)S(1)}, u32[]{:S(2)}, u32[]{:S(2)}) collective-permute-start(bf16[264,1024]{1,0:T(8,128)(2,1)} %get-tuple-element.35), channel_id=1, source_target_pairs={{0,2},{1,4},{2,3},{3,6},{4,5},{5,7},{6,0},{7,1},{8,10},{9,12},{10,... | collective-permute-start | bytes 1622024 | tf_op jit(solution)/shard_map/ppermute | solution.py:394
  68.3 38.9 %collective-permute-start.5 = (bf16[264,1024]{1,0:T(8,128)(2,1)}, bf16[264,1024]{1,0:T(8,128)(2,1)S(1)}, u32[]{:S(2)}, u32[]{:S(2)}) collective-permute-start(bf16[264,1024]{1,0:T(8,128)(2,1)} %get-tuple-element.36), channel_id=1, source_target_pairs={{0,6},{1,7},{2,0},{3,2},{4,1},{5,4},{6,3},{7,5},{8,14},{9,15},{10,... | collective-permute-start | bytes 1622024 | tf_op jit(solution)/shard_map/ppermute | solution.py:394
  107.2 25.3 %collective-permute-start.7 = (bf16[256,256]{1,0:T(8,128)(2,1)}, bf16[256,256]{1,0:T(8,128)(2,1)S(1)}, u32[]{:S(2)}, u32[]{:S(2)}) collective-permute-start(bf16[256,256]{1,0:T(8,128)(2,1)} %get-tuple-element.38), channel_id=1, source_target_pairs={{0,2},{1,4},{2,3},{3,6},{4,5},{5,7},{6,0},{7,1},{8,10},{9,12},{10,... | collective-permute-start | bytes 393224 | tf_op jit(solution)/shard_map/ppermute | solution.py:394
  108.6 23.9 %collective-permute-start.8 = (bf16[256,256]{1,0:T(8,128)(2,1)}, bf16[256,256]{1,0:T(8,128)(2,1)S(1)}, u32[]{:S(2)}, u32[]{:S(2)}) collective-permute-start(bf16[256,256]{1,0:T(8,128)(2,1)} %get-tuple-element.40), channel_id=1, source_target_pairs={{0,4},{1,3},{2,5},{3,7},{4,6},{5,0},{6,1},{7,2},{8,12},{9,11},{10,... | collective-permute-start | bytes 393224 | tf_op jit(solution)/shard_map/ppermute | solution.py:394
  110.6 22.0 %collective-permute-start.9 = (bf16[256,256]{1,0:T(8,128)(2,1)}, bf16[256,256]{1,0:T(8,128)(2,1)S(1)}, u32[]{:S(2)}, u32[]{:S(2)}) collective-permute-start(bf16[256,256]{1,0:T(8,128)(2,1)} %get-tuple-element.42), channel_id=1, source_target_pairs={{0,3},{1,5},{2,6},{3,0},{4,7},{5,1},{6,2},{7,4},{8,11},{9,13},{10,... | collective-permute-start | bytes 393224 | tf_op jit(solution)/shard_map/ppermute | solution.py:394
  111.9 20.6 %collective-permute-start.10 = (bf16[256,256]{1,0:T(8,128)(2,1)}, bf16[256,256]{1,0:T(8,128)(2,1)S(1)}, u32[]{:S(2)}, u32[]{:S(2)}) collective-permute-start(bf16[256,256]{1,0:T(8,128)(2,1)} %get-tuple-element.44), channel_id=1, source_target_pairs={{0,5},{1,6},{2,7},{3,1},{4,0},{5,2},{6,4},{7,3},{8,13},{9,14},{10,... | collective-permute-start | bytes 393224 | tf_op jit(solution)/shard_map/ppermute | solution.py:394
  113.6 19.0 %collective-permute-start.11 = (bf16[256,256]{1,0:T(8,128)(2,1)}, bf16[256,256]{1,0:T(8,128)(2,1)S(1)}, u32[]{:S(2)}, u32[]{:S(2)}) collective-permute-start(bf16[256,256]{1,0:T(8,128)(2,1)} %get-tuple-element.46), channel_id=1, source_target_pairs={{0,6},{1,7},{2,0},{3,2},{4,1},{5,4},{6,3},{7,5},{8,14},{9,15},{10,... | collective-permute-start | bytes 393224 | tf_op jit(solution)/shard_map/ppermute | solution.py:394
where the time goes:
time: 142 us; the launch traced here: 140 us
  waiting for transfers between devices  89.1 us (63%)
  Pallas kernels  32.8 us (23%)
  starting transfers between devices  14.9 us (10%)
  local copies, waits for them, and re-layouts  3.58 us (3%)
    ppermute x12, waiting for transfers between devices, send(): return lax.ppermute(message, 'ctx', pairs)  89.1 us
    pallas_call x2, Pallas kernels, per_device(): pl.pallas_call(functools.partial(mixer_kernel, peers, rows, heads, chunk,...  24.5 us
    ppermute x12, starting transfers between devices, send(): return lax.ppermute(message, 'ctx', pairs)  14.9 us
    pallas_call x2, Pallas kernels, pack(): pl.pallas_call(functools.partial(pack_kernel, peers, span, widths, heads,...  8.3 us
  transfers between devices with their start and end apart: 12, of which 3 were waited for; matrix products, arithmetic and copies ran while one was open for 2% of the time, Pallas kernels for 14%

commit v1 on v0

--- a/solution.py
+++ b/solution.py
@@ -140,20 +140,32 @@
         left_ref, b_ref = take(2)
         inward_refs = take(len(later))
         outward_refs = take(len(later))
-    wide, carry = take(2)
-    if final:
-        (total_ref,) = take(1)
+    wide, carry, x_ref, scaled_ref, scales, expand = take(6)
     if first:
-        (scalars,) = take(1)
+        scalars, ones, eye = take(3)
     blocks = rows // BLOCK
     step = pl.program_id(0)
     scale_rows = rows + 16 * blocks
     base = pl.multiple_of(step * rows, rows)
     scale_base = pl.multiple_of(step * scale_rows, 32)
 
+    def spread(count):
+        head_of = lax.broadcasted_iota(jnp.int32, (2 * count, count * HEAD_DIM), 1) // HEAD_DIM
+        row = lax.rem(
+            lax.broadcasted_iota(jnp.int32, (2 * count, count * HEAD_DIM), 0), count
+        )
+        return jnp.where(head_of == row, 1.0, 0.0).astype(jnp.bfloat16)
+
     @pl.when(step == 0)
     def _():
         carry[...] = jnp.zeros_like(carry)
+        expand[...] = spread(width // HEAD_DIM)
+        if first:
+            row = lax.broadcasted_iota(jnp.int32, (rows, rows), 0)
+            col = lax.broadcasted_iota(jnp.int32, (rows, rows), 1)
+            lower = (row >= col) & (row // BLOCK == col // BLOCK)
+            ones[...] = jnp.where(lower, 1.0, 0.0).astype(jnp.bfloat16)
+            eye[...] = jnp.where(row == col, 1.0, 0.0).astype(jnp.bfloat16)
         wide[rows : rows + HALO] = jnp.zeros((HALO, wide.shape[1]), jnp.bfloat16)
 
     wide[0:HALO] = wide[rows : rows + HALO]
@@ -168,37 +180,16 @@
             else:
                 wide[HALO : HALO + rows] = parts[k][0:rows, parts[k].shape[1] - width :]
 
-    def spread(count):
-        head_of = lax.broadcasted_iota(jnp.int32, (2 * count, count * HEAD_DIM), 1) // HEAD_DIM
-        row = lax.rem(
-            lax.broadcasted_iota(jnp.int32, (2 * count, count * HEAD_DIM), 0), count
-        )
-        return jnp.where(head_of == row, 1.0, 0.0).astype(jnp.bfloat16)
-
-    def activated(top, size, lo, hi):
-        rows_out = []
-        for r in range(top, top + size, STRIP):
-            lanes_out = []
-            for lane in range(lo, hi, LANES):
-                tap = [taps_ref[k : k + 1, lane : lane + LANES] for k in range(KW)]
-                now = wide[r : r + STRIP + HALO, lane : lane + LANES].astype(jnp.float32)[HALO // 2 :]
-                before = pltpu.roll(now, 1, 0)
-                older = pltpu.roll(tap[0] * before + tap[1] * now, 2, 0)
-                summed = (older + (tap[2] * before + tap[3] * now))[HALO // 2 :]
-                lanes_out.append(
-                    summed * pltpu.reciprocal(1.0 + jnp.exp(-summed), approx=True)
-                )
-            rows_out.append(jnp.concatenate(lanes_out, axis=1))
-        return jnp.concatenate(rows_out, axis=0)
+    def activated(r, lane):
+        tap = [taps_ref[k : k + 1, lane : lane + LANES] for k in range(KW)]
+        now = wide[r : r + STRIP + HALO, lane : lane + LANES].astype(jnp.float32)[HALO // 2 :]
+        before = pltpu.roll(now, 1, 0)
+        older = pltpu.roll(tap[0] * before + tap[1] * now, 2, 0)
+        summed = (older + (tap[2] * before + tap[3] * now))[HALO // 2 :]
+        return summed * pltpu.reciprocal(1.0 + jnp.exp(-summed), approx=True)
 
     if first:
         full = width + 2 * STATE
-        row = lax.broadcasted_iota(jnp.int32, (rows, rows), 0)
-        col = lax.broadcasted_iota(jnp.int32, (rows, rows), 1)
-        lower = (row >= col) & (row // BLOCK == col // BLOCK)
-        ones = jnp.where(lower, 1.0, 0.0).astype(jnp.bfloat16)
-        eye = jnp.where(row == col, 1.0, 0.0).astype(jnp.bfloat16)
-
         def field(p):
             pieces = [
                 scalars[top : top + count, left : left + rows].astype(jnp.float32)
@@ -207,8 +198,8 @@
             ]
             return jnp.concatenate(pieces, axis=0).astype(jnp.bfloat16)
 
-        cumul = contract(ones, field(0), ((1,), (1,)))
-        steps = contract(eye, field(1), ((1,), (1,)))
+        cumul = contract(ones[...], field(0), ((1,), (1,)))
+        steps = contract(eye[...], field(1), ((1,), (1,)))
         middles = [
             cumul[b * BLOCK + BLOCK // 2 - 1 : b * BLOCK + BLOCK // 2] for b in range(blocks)
         ]
@@ -228,10 +219,14 @@
             end = begin + widths[index] // HEAD_DIM
             return jnp.concatenate([half[:, begin:end] for half in halves], axis=1)
 
-        bc = activated(0, rows, width, full).astype(jnp.bfloat16)
-        b_part, c_part = bc[:, :STATE], bc[:, STATE:]
+        b_part, c_part = (
+            jnp.concatenate(
+                [activated(r, lane) for r in range(0, rows, STRIP)], axis=0
+            ).astype(jnp.bfloat16)
+            for lane in (width, width + STATE)
+        )
         scores = contract(c_part, b_part, ((1,), (1,)))
-        scores = jnp.where(lower, scores, 0.0).astype(jnp.bfloat16)
+        scores = jnp.where(ones[...] > 0, scores, 0.0).astype(jnp.bfloat16)
         lefts = [
             jnp.concatenate(
                 [
@@ -257,60 +252,52 @@
         b_part = b_ref[pl.ds(base, rows)]
         lefts = [left_ref[pl.ds(base + b * BLOCK, BLOCK)] for b in range(blocks)]
 
-    tile = 2 * LANES if width % (2 * LANES) == 0 else LANES
-    expand = spread(width // HEAD_DIM)
-    compact = [
-        jnp.concatenate(
-            [
-                inward[b * BLOCK : (b + 1) * BLOCK],
-                outward[b * BLOCK : (b + 1) * BLOCK],
-                outward[rows + 16 * b : rows + 16 * (b + 1)],
-            ],
-            axis=0,
-        )
-        for b in range(blocks)
-    ]
+    scales[...] = contract(
+        jnp.concatenate([inward, outward], axis=0), expand[...], ((1,), (0,))
+    )
+    for lane in range(0, width, LANES):
+        at = slice(lane, lane + LANES)
+        for r in range(0, rows, STRIP):
+            x_conv = activated(r, lane)
+            x_ref[r : r + STRIP, at] = x_conv
+            scaled_ref[r : r + STRIP, at] = (x_conv * scales[r : r + STRIP, at]).astype(
+                jnp.bfloat16
+            )
+    held = []
     for b in range(blocks):
-        top = b * BLOCK
-        power = jnp.zeros((BLOCK, LANES), jnp.float32)
-        if not first:
-            power = power_ref[pl.ds(base + top, BLOCK)]
-        for lo in range(0, width, tile):
-            hi = lo + tile
-            x_conv = activated(top, BLOCK, lo, hi)
-            scales = contract(compact[b], expand[:, lo:hi], ((1,), (0,)))
-            in_scale = scales[:BLOCK]
-            out_scale = scales[BLOCK : 2 * BLOCK]
-            mid_scale = scales[2 * BLOCK :]
-            scaled = (x_conv * in_scale).astype(jnp.bfloat16)
-            held = carry[:, lo:hi] * mid_scale[0:1]
-            right = jnp.concatenate([scaled, held.astype(jnp.bfloat16)], axis=0)
-            mixed = contract(lefts[b], right, ((1,), (0,)))
-            total = mixed * out_scale + skip_ref[0:1, lo:hi] * x_conv
-            if final:
-                total_ref[top : top + BLOCK, lo:hi] = total
-            else:
-                total_ref[pl.ds(base + top, BLOCK), lo:hi] = total.astype(jnp.bfloat16)
-            squares = total * total
-            for lane in range(0, tile, LANES):
-                power = power + squares[:, lane : lane + LANES]
-            added = contract(b_part[top : top + BLOCK], scaled, ((0,), (0,)))
-            carry[:, lo:hi] = (held + added) * out_scale[BLOCK - 1 : BLOCK]
+        at = slice(b * BLOCK, (b + 1) * BLOCK)
+        added = contract(b_part[at], scaled_ref[at], ((0,), (0,)))
+        middle_row = 2 * rows + 16 * b
+        last_row = rows + (b + 1) * BLOCK - 1
+        now = carry[...] * scales[middle_row : middle_row + 1]
+        held.append(now.astype(jnp.bfloat16))
+        carry[...] = (now + added) * scales[last_row : last_row + 1]
+    for b in range(blocks):
+        at = slice(b * BLOCK, (b + 1) * BLOCK)
+        right = jnp.concatenate([scaled_ref[at], held[b]], axis=0)
+        total = contract(lefts[b], right, ((1,), (0,)))
+        total = total * scales[rows + b * BLOCK : rows + (b + 1) * BLOCK]
+        total = total + skip_ref[...] * x_ref[at]
+        power = power_ref[pl.ds(base + b * BLOCK, BLOCK)] if not first else None
+        for lane in range(0, width, LANES):
+            square = total[:, lane : lane + LANES] * total[:, lane : lane + LANES]
+            power = square if power is None else power + square
         if final:
             summed = jnp.sum(power, axis=1, keepdims=True)
             norm = lax.rsqrt(summed * (1.0 / GROUP_WIDTH) + EPS)
             column = 0
             for index, size in enumerate(widths):
                 if index < chunk:
-                    block = earlier[index][pl.ds(base + top, BLOCK)].astype(jnp.float32)
+                    block = earlier[index][pl.ds(base + b * BLOCK, BLOCK)].astype(jnp.float32)
                 else:
-                    block = total_ref[top : top + BLOCK]
-                out_ref[top : top + BLOCK, column : column + size] = (
+                    block = total
+                out_ref[at, column : column + size] = (
                     block * norm * gain_ref[0:1, column : column + size]
                 ).astype(jnp.bfloat16)
                 column += size
         else:
-            sums_ref[pl.ds(base + top, BLOCK)] = power
+            total_ref[pl.ds(base + b * BLOCK, BLOCK)] = total.astype(jnp.bfloat16)
+            sums_ref[pl.ds(base + b * BLOCK, BLOCK)] = power
 
 
 def per_device(inputs, key_query, conv_inputs, conv_kq, step_size, decay_log, skip_gain, norm_gain):
@@ -457,11 +444,14 @@
         scratch = [
             pltpu.VMEM((rows + HALO, cols), jnp.bfloat16),
             pltpu.VMEM((STATE, width), jnp.float32),
+            pltpu.VMEM((rows, width), jnp.float32),
+            pltpu.VMEM((rows, width), jnp.bfloat16),
+            pltpu.VMEM((2 * rows + 16 * blocks, width), jnp.float32),
+            pltpu.VMEM((2 * width // HEAD_DIM, width), jnp.bfloat16),
         ]
-        if final:
-            scratch.append(pltpu.VMEM((rows, width), jnp.float32))
         if first:
             scratch.append(pltpu.VMEM((scalar_rows, cols), jnp.bfloat16))
+            scratch += [pltpu.VMEM((rows, rows), jnp.bfloat16)] * 2
         results = pl.pallas_call(
             functools.partial(mixer_kernel, peers, rows, heads, chunk, widths, whole_group),
             grid=(peers,),

time: 142 us -> 137 us (0.965)
  Pallas kernels: 32.8 us -> 28.1 us
    pallas_call x2, Pallas kernels: 24.5 us -> 19.8 us  [per_device(): pl.pallas_call(functools.partial(mixer_kernel, peers, rows, heads, chunk,...]
  transfers between devices with their start and end apart: 12 -> 12, of which waited for: 3 -> 4; matrix products, arithmetic and copies ran while one was open for 2% -> 2% of each run, Pallas kernels for 14% -> 11%
where the time goes in v1:
time: 137 us; the launch traced here: 136 us
  waiting for transfers between devices  89.4 us (65%)
  Pallas kernels  28.1 us (21%)
  starting transfers between devices  14.9 us (11%)
  local copies, waits for them, and re-layouts  3.58 us (3%)
    ppermute x12, waiting for transfers between devices, send(): return lax.ppermute(message, 'ctx', pairs)  89.4 us
    pallas_call x2, Pallas kernels, per_device(): pl.pallas_call(functools.partial(mixer_kernel, peers, rows, heads, chunk,...  19.8 us
    ppermute x12, starting transfers between devices, send(): return lax.ppermute(message, 'ctx', pairs)  14.9 us
    pallas_call x2, Pallas kernels, pack(): pl.pallas_call(functools.partial(pack_kernel, peers, span, widths, heads,...  8.3 us
  transfers between devices with their start and end apart: 12, of which 4 were waited for; matrix products, arithmetic and copies ran while one was open for 2% of the time, Pallas kernels for 11%

profile of v1, /device:TPU:12, one launch (start us, length us, event | category | flops | bytes accessed | tf_op | source)
XLA Modules:
  0.0 136.1 jit_solution(3442446748349073760)
XLA Ops:
  0.0 0.0 copy-start
  0.0 0.0 copy-start.2
  0.0 1.2 fusion.1.refs_0_
  1.3 5.5 %pack.2 = (bf16[264,1024]{1,0:T(8,128)(2,1)}, bf16[264,1024]{1,0:T(8,128)(2,1)}, bf16[264,1024]{1,0:T(8,128)(2,1)}, bf16[264,1024]{1,0:T(8,128)(2,1)}, bf16[264,...) custom-call(s32[8]{0:T(128)} %fusion.1.refs_0_, ...), custom_call_target="tpu_custom_call" | custom-call | bytes 9461760 | tf_op jit(solution)/shard_map/pack/pallas_call | solution.py:355
  6.7 0.0 copy-start.1
  6.7 2.7 %collective-permute-start.1 = (bf16[264,1024]{1,0:T(8,128)(2,1)}, bf16[264,1024]{1,0:T(8,128)(2,1)S(1)}, u32[]{:S(2)}, u32[]{:S(2)}) collective-permute-start(bf16[264,1024]{1,0:T(8,128)(2,1)} %get-tuple-element.32), channel_id=1, source_target_pairs={{0,3},{1,5},{2,6},{3,0},{4,7},{5,1},{6,2},{7,4},{8,11},{9,13},{10,... | collective-permute-start | bytes 1622024 | tf_op jit(solution)/shard_map/ppermute | solution.py:381
  9.4 0.0 collective-permute-start.2
  9.4 0.9 collective-permute-start
  10.3 0.8 collective-permute-start.6
  11.1 1.8 %collective-permute-start.3 = (bf16[264,1024]{1,0:T(8,128)(2,1)}, bf16[264,1024]{1,0:T(8,128)(2,1)}, u32[]{:S(2)}, u32[]{:S(2)}) collective-permute-start(bf16[264,1024]{1,0:T(8,128)(2,1)} %get-tuple-element.34), channel_id=1, source_target_pairs={{0,5},{1,6},{2,7},{3,1},{4,0},{5,2},{6,4},{7,3},{8,13},{9,14},{10,... | collective-permute-start | bytes 1622024 | tf_op jit(solution)/shard_map/ppermute | solution.py:381
  12.9 0.0 copy-done.2
  12.9 0.1 dynamic_slice.25
  13.0 0.1 broadcast_in_dim.4
  13.1 0.1 broadcast_in_dim_reshape.3
  13.2 2.8 %pack.3 = (bf16[256,256]{1,0:T(8,128)(2,1)}, bf16[256,256]{1,0:T(8,128)(2,1)}, bf16[256,256]{1,0:T(8,128)(2,1)}, bf16[256,256]{1,0:T(8,128)(2,1)}, bf16[256,256]{1,0:T(8,128)(2,1)}) custom-call(s32[8]{0:T(128)} %fusion.1.refs_0_, bf16[256,8192]{1,0:T(8,128)(2,1)} %refs_1_.3), custom_call_target="tpu_custom_call" | custom-call | bytes 1310720 | tf_op jit(solution)/shard_map/pack/pallas_call | solution.py:355
  16.0 0.7 dynamic-slice.3
  16.7 17.5 %collective-permute-done.1.refs_5_ = bf16[264,1024]{1,0:T(8,128)(2,1)S(1)} collective-permute-done((bf16[264,1024]{1,0:T(8,128)(2,1)}, bf16[264,1024]{1,0:T(8,128)(2,1)S(1)}, u32[]{:S(2)}, u32[]{:S(2)}) %collective-permute-start.1) | collective-permute-done | bytes 540704 | tf_op jit(solution)/shard_map/ppermute | solution.py:381
  34.3 0.0 collective-permute-start.4
  34.3 34.0 %collective-permute-done.2.refs_4_ = bf16[264,1024]{1,0:T(8,128)(2,1)S(1)} collective-permute-done((bf16[264,1024]{1,0:T(8,128)(2,1)}, bf16[264,1024]{1,0:T(8,128)(2,1)S(1)}, u32[]{:S(2)}, u32[]{:S(2)}) %collective-permute-start.2) | collective-permute-done | bytes 540704 | tf_op jit(solution)/shard_map/ppermute | solution.py:381
  68.3 0.0 collective-permute-start.5
  68.3 0.7 fusion.refs_0_
  69.0 0.0 copy-done
  69.0 0.7 constant_dynamic-slice_fusion.2
  69.7 37.5 %collective-permute-done.3.refs_6_ = bf16[264,1024]{1,0:T(8,128)(2,1)} collective-permute-done((bf16[264,1024]{1,0:T(8,128)(2,1)}, bf16[264,1024]{1,0:T(8,128)(2,1)}, u32[]{:S(2)}, u32[]{:S(2)}) %collective-permute-start.3) | collective-permute-done | bytes 540704 | tf_op jit(solution)/shard_map/ppermute | solution.py:381
  107.2 0.0 collective-permute-done.4.refs_3_
  107.2 0.0 collective-permute-done.5.refs_7_
  107.2 0.0 collective-permute-done.refs_2_
  107.2 0.0 collective-permute-done.6.refs_8_
  107.2 1.4 %collective-permute-start.7 = (bf16[256,256]{1,0:T(8,128)(2,1)}, bf16[256,256]{1,0:T(8,128)(2,1)S(1)}, u32[]{:S(2)}, u32[]{:S(2)}) collective-permute-start(bf16[256,256]{1,0:T(8,128)(2,1)} %get-tuple-element.38), channel_id=1, source_target_pairs={{0,2},{1,4},{2,3},{3,6},{4,5},{5,7},{6,0},{7,1},{8,10},{9,12},{10,... | collective-permute-start | bytes 393224 | tf_op jit(solution)/shard_map/ppermute | solution.py:381
  108.6 1.9 %collective-permute-start.8 = (bf16[256,256]{1,0:T(8,128)(2,1)}, bf16[256,256]{1,0:T(8,128)(2,1)S(1)}, u32[]{:S(2)}, u32[]{:S(2)}) collective-permute-start(bf16[256,256]{1,0:T(8,128)(2,1)} %get-tuple-element.40), channel_id=1, source_target_pairs={{0,4},{1,3},{2,5},{3,7},{4,6},{5,0},{6,1},{7,2},{8,12},{9,11},{10,... | collective-permute-start | bytes 393224 | tf_op jit(solution)/shard_map/ppermute | solution.py:381
  110.6 1.4 %collective-permute-start.9 = (bf16[256,256]{1,0:T(8,128)(2,1)}, bf16[256,256]{1,0:T(8,128)(2,1)S(1)}, u32[]{:S(2)}, u32[]{:S(2)}) collective-permute-start(bf16[256,256]{1,0:T(8,128)(2,1)} %get-tuple-element.42), channel_id=1, source_target_pairs={{0,3},{1,5},{2,6},{3,0},{4,7},{5,1},{6,2},{7,4},{8,11},{9,13},{10,... | collective-permute-start | bytes 393224 | tf_op jit(solution)/shard_map/ppermute | solution.py:381
  111.9 1.7 %collective-permute-start.10 = (bf16[256,256]{1,0:T(8,128)(2,1)}, bf16[256,256]{1,0:T(8,128)(2,1)S(1)}, u32[]{:S(2)}, u32[]{:S(2)}) collective-permute-start(bf16[256,256]{1,0:T(8,128)(2,1)} %get-tuple-element.44), channel_id=1, source_target_pairs={{0,5},{1,6},{2,7},{3,1},{4,0},{5,2},{6,4},{7,3},{8,13},{9,14},{10,... | collective-permute-start | bytes 393224 | tf_op jit(solution)/shard_map/ppermute | solution.py:381
  113.6 2.3 %collective-permute-start.11 = (bf16[256,256]{1,0:T(8,128)(2,1)}, bf16[256,256]{1,0:T(8,128)(2,1)S(1)}, u32[]{:S(2)}, u32[]{:S(2)}) collective-permute-start(bf16[256,256]{1,0:T(8,128)(2,1)} %get-tuple-element.46), channel_id=1, source_target_pairs={{0,6},{1,7},{2,0},{3,2},{4,1},{5,4},{6,3},{7,5},{8,14},{9,15},{10,... | collective-permute-start | bytes 393224 | tf_op jit(solution)/shard_map/ppermute | solution.py:381
  115.9 0.0 copy-done.1
  115.9 12.6 %mixer0.1 = (bf16[2048,768]{1,0:T(8,128)(2,1)S(1)}, f32[2048,128]{1,0:T(8,128)S(1)}, bf16[2048,256]{1,0:T(8,128)(2,1)S(1)}, bf16[2048,128]{1,0:T(8,128)(2,1)S(1)...) custom-call(s32[8]{0:T(128)S(1)} %fusion.refs_0_, bf16[264,1280]{1,0:T(8,128)(2,1)S(1)} %copy-done.1, ...), custom_call_target="tpu_custom_call" | custom-call | flops 1415577600 | bytes 16777216 | tf_op jit(solution)/shard_map/mixer0/pallas_call | solution.py:455
  128.6 0.0 collective-permute-done.7.refs_3_
  128.6 0.0 collective-permute-done.8.refs_4_
  128.6 0.0 collective-permute-done.9.refs_5_
  128.6 0.3 collective-permute-done.10.refs_6_
  128.9 0.0 collective-permute-done.11.refs_7_
  128.9 7.2 %mixer1.1 = bf16[2048,1024]{1,0:T(8,128)(2,1)} custom-call(s32[8]{0:T(128)S(1)} %fusion.refs_0_, bf16[264,1280]{1,0:T(8,128)(2,1)S(1)} %copy-done.1, bf16[264,1280]{1,0:T(8,128)(2,1)S(1)} %collective-permute-done.refs_2_, bf16[256,256]{1,0:T(8,128)(2,1)S(1)} %collective-permute-done.7.refs_3_, bf16[256,256]{1,0:T(8,128)(2,1)S(1)} %collective-permute-done.8.refs_4_, ...), custom_call_target="tpu_custom_call" | custom-call | flops 471859200 | bytes 5242880 | tf_op jit(solution)/shard_map/mixer1/pallas_call | solution.py:455
  (5 shorter events, 0.0 us)
Async XLA Ops:
  0.0 69.0 %copy-start = (f32[4,8192]{1,0:T(4,128)S(1)}, f32[4,8192]{1,0:T(4,128)}, u32[]{:S(2)}) copy-start(f32[4,8192]{1,0:T(4,128)} %param.12) | copy-start | bytes 393220
  0.0 12.9 %copy-start.2 = (f32[128]{0:T(128)S(1)}, f32[128]{0:T(128)}, u32[]{:S(2)}) copy-start(f32[128]{0:T(128)} %param.16) | copy-start | bytes 1540
  6.7 109.2 %copy-start.1 = (bf16[264,1280]{1,0:T(8,128)(2,1)S(1)}, bf16[264,1280]{1,0:T(8,128)(2,1)}, u32[]{:S(2)}) copy-start(bf16[264,1280]{1,0:T(8,128)(2,1)} %get-tuple-element.29.refs_1_) | copy-start | bytes 2027524
  6.7 27.5 %collective-permute-start.1 = (bf16[264,1024]{1,0:T(8,128)(2,1)}, bf16[264,1024]{1,0:T(8,128)(2,1)S(1)}, u32[]{:S(2)}, u32[]{:S(2)}) collective-permute-start(bf16[264,1024]{1,0:T(8,128)(2,1)} %get-tuple-element.32), channel_id=1, source_target_pairs={{0,3},{1,5},{2,6},{3,0},{4,7},{5,1},{6,2},{7,4},{8,11},{9,13},{10,... | collective-permute-start | bytes 1622024 | tf_op jit(solution)/shard_map/ppermute | solution.py:381
  9.4 58.9 %collective-permute-start.2 = (bf16[264,1024]{1,0:T(8,128)(2,1)}, bf16[264,1024]{1,0:T(8,128)(2,1)S(1)}, u32[]{:S(2)}, u32[]{:S(2)}) collective-permute-start(bf16[264,1024]{1,0:T(8,128)(2,1)} %get-tuple-element.33), channel_id=1, source_target_pairs={{0,4},{1,3},{2,5},{3,7},{4,6},{5,0},{6,1},{7,2},{8,12},{9,11},{10,... | collective-permute-start | bytes 1622024 | tf_op jit(solution)/shard_map/ppermute | solution.py:381
  9.4 97.8 %collective-permute-start = (bf16[264,1280]{1,0:T(8,128)(2,1)}, bf16[264,1280]{1,0:T(8,128)(2,1)S(1)}, u32[]{:S(2)}, u32[]{:S(2)}) collective-permute-start(bf16[264,1280]{1,0:T(8,128)(2,1)} %get-tuple-element.30), channel_id=1, source_target_pairs={{0,1},{1,2},{2,4},{3,5},{4,3},{5,6},{6,7},{7,0},{8,9},{9,10},{10,1... | collective-permute-start | bytes 2027528 | tf_op jit(solution)/shard_map/ppermute | solution.py:381
  10.3 96.9 %collective-permute-start.6 = (bf16[264,1280]{1,0:T(8,128)(2,1)}, bf16[264,1280]{1,0:T(8,128)(2,1)S(1)}, u32[]{:S(2)}, u32[]{:S(2)}) collective-permute-start(bf16[264,1280]{1,0:T(8,128)(2,1)} %get-tuple-element.37), channel_id=1, source_target_pairs={{0,7},{1,0},{2,1},{3,4},{4,2},{5,3},{6,5},{7,6},{8,15},{9,8},{10,9... | collective-permute-start | bytes 2027528 | tf_op jit(solution)/shard_map/ppermute | solution.py:381
  11.1 96.1 %collective-permute-start.3 = (bf16[264,1024]{1,0:T(8,128)(2,1)}, bf16[264,1024]{1,0:T(8,128)(2,1)}, u32[]{:S(2)}, u32[]{:S(2)}) collective-permute-start(bf16[264,1024]{1,0:T(8,128)(2,1)} %get-tuple-element.34), channel_id=1, source_target_pairs={{0,5},{1,6},{2,7},{3,1},{4,0},{5,2},{6,4},{7,3},{8,13},{9,14},{10,... | collective-permute-start | bytes 1622024 | tf_op jit(solution)/shard_map/ppermute | solution.py:381
  34.3 73.0 %collective-permute-start.4 = (bf16[264,1024]{1,0:T(8,128)(2,1)}, bf16[264,1024]{1,0:T(8,128)(2,1)S(1)}, u32[]{:S(2)}, u32[]{:S(2)}) collective-permute-start(bf16[264,1024]{1,0:T(8,128)(2,1)} %get-tuple-element.35), channel_id=1, source_target_pairs={{0,2},{1,4},{2,3},{3,6},{4,5},{5,7},{6,0},{7,1},{8,10},{9,12},{10,... | collective-permute-start | bytes 1622024 | tf_op jit(solution)/shard_map/ppermute | solution.py:381
  68.3 38.9 %collective-permute-start.5 = (bf16[264,1024]{1,0:T(8,128)(2,1)}, bf16[264,1024]{1,0:T(8,128)(2,1)S(1)}, u32[]{:S(2)}, u32[]{:S(2)}) collective-permute-start(bf16[264,1024]{1,0:T(8,128)(2,1)} %get-tuple-element.36), channel_id=1, source_target_pairs={{0,6},{1,7},{2,0},{3,2},{4,1},{5,4},{6,3},{7,5},{8,14},{9,15},{10,... | collective-permute-start | bytes 1622024 | tf_op jit(solution)/shard_map/ppermute | solution.py:381
  107.2 21.3 %collective-permute-start.7 = (bf16[256,256]{1,0:T(8,128)(2,1)}, bf16[256,256]{1,0:T(8,128)(2,1)S(1)}, u32[]{:S(2)}, u32[]{:S(2)}) collective-permute-start(bf16[256,256]{1,0:T(8,128)(2,1)} %get-tuple-element.38), channel_id=1, source_target_pairs={{0,2},{1,4},{2,3},{3,6},{4,5},{5,7},{6,0},{7,1},{8,10},{9,12},{10,... | collective-permute-start | bytes 393224 | tf_op jit(solution)/shard_map/ppermute | solution.py:381
  108.6 19.9 %collective-permute-start.8 = (bf16[256,256]{1,0:T(8,128)(2,1)}, bf16[256,256]{1,0:T(8,128)(2,1)S(1)}, u32[]{:S(2)}, u32[]{:S(2)}) collective-permute-start(bf16[256,256]{1,0:T(8,128)(2,1)} %get-tuple-element.40), channel_id=1, source_target_pairs={{0,4},{1,3},{2,5},{3,7},{4,6},{5,0},{6,1},{7,2},{8,12},{9,11},{10,... | collective-permute-start | bytes 393224 | tf_op jit(solution)/shard_map/ppermute | solution.py:381
  110.6 18.0 %collective-permute-start.9 = (bf16[256,256]{1,0:T(8,128)(2,1)}, bf16[256,256]{1,0:T(8,128)(2,1)S(1)}, u32[]{:S(2)}, u32[]{:S(2)}) collective-permute-start(bf16[256,256]{1,0:T(8,128)(2,1)} %get-tuple-element.42), channel_id=1, source_target_pairs={{0,3},{1,5},{2,6},{3,0},{4,7},{5,1},{6,2},{7,4},{8,11},{9,13},{10,... | collective-permute-start | bytes 393224 | tf_op jit(solution)/shard_map/ppermute | solution.py:381
  111.9 16.9 %collective-permute-start.10 = (bf16[256,256]{1,0:T(8,128)(2,1)}, bf16[256,256]{1,0:T(8,128)(2,1)S(1)}, u32[]{:S(2)}, u32[]{:S(2)}) collective-permute-start(bf16[256,256]{1,0:T(8,128)(2,1)} %get-tuple-element.44), channel_id=1, source_target_pairs={{0,5},{1,6},{2,7},{3,1},{4,0},{5,2},{6,4},{7,3},{8,13},{9,14},{10,... | collective-permute-start | bytes 393224 | tf_op jit(solution)/shard_map/ppermute | solution.py:381
  113.6 15.3 %collective-permute-start.11 = (bf16[256,256]{1,0:T(8,128)(2,1)}, bf16[256,256]{1,0:T(8,128)(2,1)S(1)}, u32[]{:S(2)}, u32[]{:S(2)}) collective-permute-start(bf16[256,256]{1,0:T(8,128)(2,1)} %get-tuple-element.46), channel_id=1, source_target_pairs={{0,6},{1,7},{2,0},{3,2},{4,1},{5,4},{6,3},{7,5},{8,14},{9,15},{10,... | collective-permute-start | bytes 393224 | tf_op jit(solution)/shard_map/ppermute | solution.py:381
